TPU v7x, 256 devices: a whole 4x4x8 slice. The times are simulated.
256 devices in a mesh: slab: 64 (over z, x, core), energy: 4 (over y).
Axes of the slice: x: 4, y: 4, z: 8, core: 2. Of those that a mesh axis runs over, the one named last changes fastest.
Arguments:
- energy_sq: float32 [4], P('energy'), may hold values from 2.5 to 3.3
- broadening: float32 [4], P('energy'), may hold values from 0.05 to 0.1
- onsite: float32 [64, 192, 192], P('slab'), may hold values from -0.005051815 to 2
- coupling: float32 [64, 192, 192], P('slab'), may hold values from -0.005051815 to 0.005051815
- sigma_in: float32 [4, 64, 192, 384], P('energy', 'slab'), may hold values from -0.02 to 0.005051815
- anharmonic: float32 [64, 192, 192], P('slab'), may hold values from 0.5 to 2
- energy_pairs: int32 [4, 8, 2], P('energy'), may hold values from 0 to 3
Outputs:
- green_diag: float32 [4, 64, 192, 384], P('energy', 'slab')
- sigma_out: float32 [4, 64, 192, 384], P('energy', 'slab')
All inputs are finite; a program needn't handle non-finite values.
Results may differ from a plain program's by a relative error of at most 0.0003.
Values sent between devices are 32-bit elements; how exact they have to be, the bound alone decides.
A program may use at most 128 MiB of HBM per device.

v0:
```python
import jax
import jax.numpy as jnp
from jax import lax
from jax.sharding import PartitionSpec as P


def shifted(value, axis, steps):
    count = lax.axis_size(axis)
    first, last = (max(0, -steps), min(count, count - steps))
    return lax.ppermute(value, axis, [(source, source + steps) for source in range(first, last)])


def complex_product(left, right):
    block_width = left.shape[-2]
    high = lax.Precision.HIGHEST
    right_real = right[..., :block_width]
    right_imag = right[..., block_width:]
    stacked = jnp.concatenate(
        [
            jnp.concatenate([right_real, right_imag], -1),
            jnp.concatenate([-right_imag, right_real], -1),
        ],
        -2,
    )
    return jnp.einsum("...ij,...jk->...ik", left, stacked, precision=high)


def invert(matrix):
    block_width = matrix.shape[-2]
    high = lax.Precision.HIGHEST
    real_part = matrix[..., :block_width]
    imag_part = matrix[..., block_width:]
    real_part = 0.5 * (real_part + jnp.swapaxes(real_part, -1, -2))
    imag_part = 0.5 * (imag_part + jnp.swapaxes(imag_part, -1, -2))
    identity = jnp.broadcast_to(jnp.eye(block_width, dtype=jnp.float32), real_part.shape)
    imag_factor = jnp.linalg.cholesky(imag_part)
    factor_inverse = jax.scipy.linalg.solve_triangular(imag_factor, identity, lower=True)
    factor_trans = jnp.swapaxes(factor_inverse, -1, -2)
    middle = jnp.einsum(
        "...ij,...jk,...kl->...il", factor_inverse, real_part, factor_trans, precision=high
    )
    middle = 0.5 * (middle + jnp.swapaxes(middle, -1, -2))
    squared = jnp.einsum("...ij,...jk->...ik", middle, middle, precision=high) + identity
    square_factor = jnp.linalg.cholesky(squared)
    right_side = jax.scipy.linalg.cho_solve((square_factor, True), factor_inverse)
    first_real = jnp.einsum(
        "...ij,...jk,...kl->...il", factor_trans, middle, right_side, precision=high
    )
    first_imag = -jnp.einsum("...ij,...jk->...ik", factor_trans, right_side, precision=high)
    first = jnp.concatenate([first_real, first_imag], -1)
    first = 2.0 * first - complex_product(first, complex_product(matrix, first))
    return first


def reduce_levels(matrix, lower_block, upper_block):
    slab_count = lax.axis_size("slab")
    level_count = slab_count.bit_length() - 1
    for level_index in range(level_count):
        distance = 2**level_index
        inverse = invert(matrix)
        forward = complex_product(inverse, upper_block)
        backward = complex_product(inverse, lower_block)
        if level_index + 1 < level_count:
            payload = jnp.stack([forward, backward])
            low_side = shifted(payload, "slab", distance)
            high_side = shifted(payload, "slab", -distance)
            matrix = (
                matrix
                - complex_product(lower_block, low_side[0])
                - complex_product(upper_block, high_side[1])
            )
            new_lower = -complex_product(lower_block, low_side[1])
            new_upper = -complex_product(upper_block, high_side[0])
            lower_block = new_lower
            upper_block = new_upper
        else:
            last_payload = jnp.stack([forward, backward])
            low_pair = shifted(last_payload, "slab", distance)
            high_pair = shifted(last_payload, "slab", -distance)
            low_forward = low_pair[0]
            high_backward = high_pair[1]
            matrix = (
                matrix
                - complex_product(lower_block, low_forward)
                - complex_product(upper_block, high_backward)
            )
    return invert(matrix)


def shards(energy_sq, broadening, onsite, coupling, sigma_in, anharmonic, energy_pairs):
    block_width = onsite.shape[-1]
    energy_count = energy_sq.shape[0]
    identity = jnp.eye(block_width, dtype=jnp.float32)
    blank = jnp.zeros((block_width, block_width), jnp.float32)
    bond_block = identity + coupling[0]
    bond_below = shifted(bond_block, "slab", 1)
    upper_one = jnp.concatenate([-bond_block, blank], -1)
    lower_one = jnp.concatenate([-bond_below.T, blank], -1)
    self_part = sigma_in[:, 0]
    diag_real = (
        energy_sq[:, None, None] * identity[None] - onsite[0][None] - self_part[..., :block_width]
    )
    diag_imag = broadening[:, None, None] * identity[None] - self_part[..., block_width:]
    matrix = jnp.concatenate([diag_real, diag_imag], -1)
    upper_all = jnp.broadcast_to(upper_one, (energy_count, block_width, 2 * block_width))
    lower_all = jnp.broadcast_to(lower_one, (energy_count, block_width, 2 * block_width))
    green_local = reduce_levels(matrix, lower_all, upper_all)
    everyone = lax.all_gather(green_local[:, None], "energy", axis=0, tiled=True)[:, 0]
    pair_count = energy_pairs.shape[1]
    first = jnp.take(everyone, energy_pairs[:, :, 0], axis=0)
    second = jnp.take(everyone, energy_pairs[:, :, 1], axis=0)
    real_part = (
        first[..., :block_width] * second[..., :block_width]
        - first[..., block_width:] * second[..., block_width:]
    )
    imag_part = (
        first[..., :block_width] * second[..., block_width:]
        + first[..., block_width:] * second[..., :block_width]
    )
    summed_real = jnp.sum(real_part, axis=1)
    summed_imag = jnp.sum(imag_part, axis=1)
    scale = anharmonic[0] / pair_count
    sigma_local = jnp.concatenate([summed_real * scale[None], summed_imag * scale[None]], -1)
    return (green_local[:, None], sigma_local[:, None])


def solution(mesh):
    in_specs = (
        P("energy"),
        P("energy"),
        P("slab", None, None),
        P("slab", None, None),
        P("energy", "slab", None, None),
        P("slab", None, None),
        P("energy", None, None),
    )
    out_specs = (P("energy", "slab", None, None), P("energy", "slab", None, None))
    return jax.shard_map(shards, mesh=mesh, in_specs=in_specs, out_specs=out_specs, check_vma=False)
```

profile of v0, /device:TPU:2, one launch (start us, length us, event | category | flops | bytes accessed | tf_op | source)
XLA Modules:
  0.0 1013.1 jit_solution(17196710646150836668)
XLA Ops:
  13.4 11.7 %custom-call.81 = f32[1,128,128]{2,1,0:T(8,128)S(1)} custom-call(f32[1,128,128]{2,1,0:T(8,128)S(1)} %copy.15), custom_call_target="Cholesky" | custom-call | tf_op jit(solution)/shard_map/jit(cholesky)/cholesky | solution.py:36
  44.1 19.9 %custom-call.84 = f32[2,128,128]{1,2,0:T(8,128)S(1)} custom-call(f32[2,128,128]{2,1,0:T(8,128)S(1)} %pad_maximum_fusion.34), custom_call_target="InvertDiagBlocksLowerTriangular" | custom-call | tf_op jit(solution)/shard_map/jit(_solve_triangular)/triangular_solve/custom-call.1 | solution.py:37
  66.9 11.7 %custom-call.85 = f32[1,128,128]{2,1,0:T(8,128)S(1)} custom-call(f32[1,128,128]{2,1,0:T(8,128)S(1)} %cholesky.1192), custom_call_target="Cholesky" | custom-call | tf_op jit(solution)/shard_map/jit(cholesky)/cholesky | solution.py:44
  97.5 20.1 %custom-call.88 = f32[2,128,128]{1,2,0:T(8,128)S(1)} custom-call(f32[2,128,128]{2,1,0:T(8,128)S(1)} %pad_maximum_fusion.35), custom_call_target="InvertDiagBlocksLowerTriangular" | custom-call | tf_op jit(solution)/shard_map/jit(_cho_solve)/triangular_solve | solution.py:45
  141.4 11.7 %custom-call.90 = f32[1,128,128]{2,1,0:T(8,128)S(1)} custom-call(f32[1,128,128]{2,1,0:T(8,128)S(1)} %copy.29), custom_call_target="Cholesky" | custom-call | tf_op jit(solution)/shard_map/jit(cholesky)/cholesky | solution.py:36
  172.3 19.9 %custom-call.93 = f32[2,128,128]{1,2,0:T(8,128)S(1)} custom-call(f32[2,128,128]{2,1,0:T(8,128)S(1)} %pad_maximum_fusion.36), custom_call_target="InvertDiagBlocksLowerTriangular" | custom-call | tf_op jit(solution)/shard_map/jit(_solve_triangular)/triangular_solve/custom-call.1 | solution.py:37
  195.1 11.7 %custom-call.94 = f32[1,128,128]{2,1,0:T(8,128)S(1)} custom-call(f32[1,128,128]{2,1,0:T(8,128)S(1)} %cholesky.1198), custom_call_target="Cholesky" | custom-call | tf_op jit(solution)/shard_map/jit(cholesky)/cholesky | solution.py:44
  225.7 20.1 %custom-call.97 = f32[2,128,128]{1,2,0:T(8,128)S(1)} custom-call(f32[2,128,128]{2,1,0:T(8,128)S(1)} %pad_maximum_fusion.37), custom_call_target="InvertDiagBlocksLowerTriangular" | custom-call | tf_op jit(solution)/shard_map/jit(_cho_solve)/triangular_solve | solution.py:45
  274.9 11.7 %custom-call.99 = f32[1,128,128]{2,1,0:T(8,128)S(1)} custom-call(f32[1,128,128]{2,1,0:T(8,128)S(1)} %copy.43), custom_call_target="Cholesky" | custom-call | tf_op jit(solution)/shard_map/jit(cholesky)/cholesky | solution.py:36
  305.8 19.9 %custom-call.102 = f32[2,128,128]{1,2,0:T(8,128)S(1)} custom-call(f32[2,128,128]{2,1,0:T(8,128)S(1)} %pad_maximum_fusion.38), custom_call_target="InvertDiagBlocksLowerTriangular" | custom-call | tf_op jit(solution)/shard_map/jit(_solve_triangular)/triangular_solve/custom-call.1 | solution.py:37
  328.5 11.7 %custom-call.103 = f32[1,128,128]{2,1,0:T(8,128)S(1)} custom-call(f32[1,128,128]{2,1,0:T(8,128)S(1)} %cholesky.1204), custom_call_target="Cholesky" | custom-call | tf_op jit(solution)/shard_map/jit(cholesky)/cholesky | solution.py:44
  359.1 20.1 %custom-call.106 = f32[2,128,128]{1,2,0:T(8,128)S(1)} custom-call(f32[2,128,128]{2,1,0:T(8,128)S(1)} %pad_maximum_fusion.39), custom_call_target="InvertDiagBlocksLowerTriangular" | custom-call | tf_op jit(solution)/shard_map/jit(_cho_solve)/triangular_solve | solution.py:45
  407.3 12.6 %collective-permute-done.5 = f32[2,1,192,384]{3,2,1,0:T(8,128)S(1)} collective-permute-done((f32[2,1,192,384]{3,2,1,0:T(8,128)S(1)}, f32[2,1,192,384]{3,2,1,0:T(8,128)S(1)}, u32[]{:S(2)}, u32[]{:S(2)}) %collective-permute-start.5) | collective-permute-done | bytes 589856 | tf_op jit(solution)/shard_map/ppermute | solution.py:10
  422.3 11.7 %custom-call.108 = f32[1,128,128]{2,1,0:T(8,128)S(1)} custom-call(f32[1,128,128]{2,1,0:T(8,128)S(1)} %copy.57), custom_call_target="Cholesky" | custom-call | tf_op jit(solution)/shard_map/jit(cholesky)/cholesky | solution.py:36
  453.2 19.9 %custom-call.111 = f32[2,128,128]{1,2,0:T(8,128)S(1)} custom-call(f32[2,128,128]{2,1,0:T(8,128)S(1)} %pad_maximum_fusion.40), custom_call_target="InvertDiagBlocksLowerTriangular" | custom-call | tf_op jit(solution)/shard_map/jit(_solve_triangular)/triangular_solve/custom-call.1 | solution.py:37
  476.0 11.7 %custom-call.112 = f32[1,128,128]{2,1,0:T(8,128)S(1)} custom-call(f32[1,128,128]{2,1,0:T(8,128)S(1)} %cholesky.1210), custom_call_target="Cholesky" | custom-call | tf_op jit(solution)/shard_map/jit(cholesky)/cholesky | solution.py:44
  506.6 20.1 %custom-call.115 = f32[2,128,128]{1,2,0:T(8,128)S(1)} custom-call(f32[2,128,128]{2,1,0:T(8,128)S(1)} %pad_maximum_fusion.41), custom_call_target="InvertDiagBlocksLowerTriangular" | custom-call | tf_op jit(solution)/shard_map/jit(_cho_solve)/triangular_solve | solution.py:45
  555.8 11.7 %custom-call.117 = f32[1,128,128]{2,1,0:T(8,128)S(1)} custom-call(f32[1,128,128]{2,1,0:T(8,128)S(1)} %copy.71), custom_call_target="Cholesky" | custom-call | tf_op jit(solution)/shard_map/jit(cholesky)/cholesky | solution.py:36
  586.7 19.9 %custom-call.120 = f32[2,128,128]{1,2,0:T(8,128)S(1)} custom-call(f32[2,128,128]{2,1,0:T(8,128)S(1)} %pad_maximum_fusion.42), custom_call_target="InvertDiagBlocksLowerTriangular" | custom-call | tf_op jit(solution)/shard_map/jit(_solve_triangular)/triangular_solve/custom-call.1 | solution.py:37
  609.5 11.7 %custom-call.121 = f32[1,128,128]{2,1,0:T(8,128)S(1)} custom-call(f32[1,128,128]{2,1,0:T(8,128)S(1)} %cholesky.1216), custom_call_target="Cholesky" | custom-call | tf_op jit(solution)/shard_map/jit(cholesky)/cholesky | solution.py:44
  640.1 20.1 %custom-call.124 = f32[2,128,128]{1,2,0:T(8,128)S(1)} custom-call(f32[2,128,128]{2,1,0:T(8,128)S(1)} %pad_maximum_fusion.43), custom_call_target="InvertDiagBlocksLowerTriangular" | custom-call | tf_op jit(solution)/shard_map/jit(_cho_solve)/triangular_solve | solution.py:45
  680.1 23.0 %collective-permute-done.10 = f32[2,1,192,384]{3,2,1,0:T(8,128)S(1)} collective-permute-done((f32[2,1,192,384]{3,2,1,0:T(8,128)S(1)}, f32[2,1,192,384]{3,2,1,0:T(8,128)S(1)}, u32[]{:S(2)}, u32[]{:S(2)}) %collective-permute-start.10) | collective-permute-done | bytes 589856 | tf_op jit(solution)/shard_map/ppermute | solution.py:10
  705.6 11.7 %custom-call.126 = f32[1,128,128]{2,1,0:T(8,128)S(1)} custom-call(f32[1,128,128]{2,1,0:T(8,128)S(1)} %copy.85), custom_call_target="Cholesky" | custom-call | tf_op jit(solution)/shard_map/jit(cholesky)/cholesky | solution.py:36
  736.5 19.9 %custom-call.129 = f32[2,128,128]{1,2,0:T(8,128)S(1)} custom-call(f32[2,128,128]{2,1,0:T(8,128)S(1)} %pad_maximum_fusion.44), custom_call_target="InvertDiagBlocksLowerTriangular" | custom-call | tf_op jit(solution)/shard_map/jit(_solve_triangular)/triangular_solve/custom-call.1 | solution.py:37
  759.3 11.7 %custom-call.130 = f32[1,128,128]{2,1,0:T(8,128)S(1)} custom-call(f32[1,128,128]{2,1,0:T(8,128)S(1)} %cholesky.1222), custom_call_target="Cholesky" | custom-call | tf_op jit(solution)/shard_map/jit(cholesky)/cholesky | solution.py:44
  789.9 20.1 %custom-call.133 = f32[2,128,128]{1,2,0:T(8,128)S(1)} custom-call(f32[2,128,128]{2,1,0:T(8,128)S(1)} %pad_maximum_fusion.45), custom_call_target="InvertDiagBlocksLowerTriangular" | custom-call | tf_op jit(solution)/shard_map/jit(_cho_solve)/triangular_solve | solution.py:45
  819.5 12.9 %collective-permute-start.11 = (f32[2,1,192,384]{3,2,1,0:T(8,128)S(1)}, f32[2,1,192,384]{3,2,1,0:T(8,128)S(1)}, u32[]{:S(2)}, u32[]{:S(2)}) collective-permute-start(f32[2,1,192,384]{3,2,1,0:T(8,128)S(1)} %pad_maximum_fusion.5), channel_id=1, source_target_pairs={{0,128},{4,132},{8,136},{12,140},{16,144},{20,148},{24,152},{28,15... | collective-permute-start | bytes 1769480 | tf_op jit(solution)/shard_map/ppermute | solution.py:10
  841.8 13.5 %collective-permute-done.11 = f32[2,1,192,384]{3,2,1,0:T(8,128)S(1)} collective-permute-done((f32[2,1,192,384]{3,2,1,0:T(8,128)S(1)}, f32[2,1,192,384]{3,2,1,0:T(8,128)S(1)}, u32[]{:S(2)}, u32[]{:S(2)}) %collective-permute-start.11) | collective-permute-done | bytes 589856 | tf_op jit(solution)/shard_map/ppermute | solution.py:10
  857.7 11.7 %custom-call.135 = f32[1,128,128]{2,1,0:T(8,128)S(1)} custom-call(f32[1,128,128]{2,1,0:T(8,128)S(1)} %cholesky.1225), custom_call_target="Cholesky" | custom-call | tf_op jit(solution)/shard_map/jit(cholesky)/cholesky | solution.py:36
  888.4 19.9 %custom-call.138 = f32[2,128,128]{1,2,0:T(8,128)S(1)} custom-call(f32[2,128,128]{2,1,0:T(8,128)S(1)} %pad_maximum_fusion.46), custom_call_target="InvertDiagBlocksLowerTriangular" | custom-call | tf_op jit(solution)/shard_map/jit(_solve_triangular)/triangular_solve/custom-call.1 | solution.py:37
  941.5 19.9 %custom-call.142 = f32[2,128,128]{1,2,0:T(8,128)S(1)} custom-call(f32[2,128,128]{2,1,0:T(8,128)S(1)} %pad_maximum_fusion.47), custom_call_target="InvertDiagBlocksLowerTriangular" | custom-call | tf_op jit(solution)/shard_map/jit(_cho_solve)/triangular_solve | solution.py:45
  966.8 30.9 %all-gather.3.cloned.1.call-done = f32[768,384]{1,0:T(8,128)} async-done(((f32[192,384]{1,0:T(8,128)}), f32[768,384]{1,0:T(8,128)}) %all-gather.3.cloned.1.call-update) | async-done | bytes 1179664 | tf_op jit(solution)/shard_map/all_gather | solution.py:108
  (561 shorter events, 450.8 us)
Async XLA Ops:
  7.2 990.5 %all-gather.3.cloned.1.call-start = ((), (), s32[]{:S(2)}) async-start(), calls=%async_computation | async-start | bytes 1474560 | tf_op jit(solution)/shard_map/all_gather | solution.py:108
  8.3 114.7 %collective-permute-start = (f32[192,192]{0,1:T(8,128)S(1)}, f32[192,192]{0,1:T(8,128)S(1)}, u32[]{:S(2)}, u32[]{:S(2)}) collective-permute-start(f32[192,192]{0,1:T(8,128)S(1)} %get-tuple-element.293), channel_id=1, source_target_pairs={{0,4},{4,8},{8,12},{12,16},{16,20},{20,24},{24,28},{28,32},{32,36}... | collective-permute-start | bytes 442376 | tf_op jit(solution)/shard_map/ppermute | solution.py:10
  124.1 11.0 %collective-permute-start.2 = (f32[2,1,192,384]{3,2,1,0:T(8,128)S(1)}, f32[2,1,192,384]{3,2,1,0:T(8,128)S(1)}, u32[]{:S(2)}, u32[]{:S(2)}) collective-permute-start(f32[2,1,192,384]{3,2,1,0:T(8,128)S(1)} %pad_maximum_fusion), channel_id=1, source_target_pairs={{4,0},{8,4},{12,8},{16,12},{20,16},{24,20},{28,24},{32,28},{36,32}... | collective-permute-start | bytes 1769480 | tf_op jit(solution)/shard_map/ppermute | solution.py:10
  127.7 11.2 %collective-permute-start.1 = (f32[2,1,192,384]{3,2,1,0:T(8,128)S(1)}, f32[2,1,192,384]{3,2,1,0:T(8,128)S(1)}, u32[]{:S(2)}, u32[]{:S(2)}) collective-permute-start(f32[2,1,192,384]{3,2,1,0:T(8,128)S(1)} %pad_maximum_fusion), channel_id=1, source_target_pairs={{0,4},{4,8},{8,12},{12,16},{16,20},{20,24},{24,28},{28,32},{32,36}... | collective-permute-start | bytes 1769480 | tf_op jit(solution)/shard_map/ppermute | solution.py:10
  254.1 16.3 %collective-permute-start.4 = (f32[2,1,192,384]{3,2,1,0:T(8,128)S(1)}, f32[2,1,192,384]{3,2,1,0:T(8,128)S(1)}, u32[]{:S(2)}, u32[]{:S(2)}) collective-permute-start(f32[2,1,192,384]{3,2,1,0:T(8,128)S(1)} %pad_maximum_fusion.1), channel_id=1, source_target_pairs={{8,0},{12,4},{16,8},{20,12},{24,16},{28,20},{32,24},{36,28},{40,32... | collective-permute-start | bytes 1769480 | tf_op jit(solution)/shard_map/ppermute | solution.py:10
  256.0 16.5 %collective-permute-start.3 = (f32[2,1,192,384]{3,2,1,0:T(8,128)S(1)}, f32[2,1,192,384]{3,2,1,0:T(8,128)S(1)}, u32[]{:S(2)}, u32[]{:S(2)}) collective-permute-start(f32[2,1,192,384]{3,2,1,0:T(8,128)S(1)} %pad_maximum_fusion.1), channel_id=1, source_target_pairs={{0,8},{4,12},{8,16},{12,20},{16,24},{20,28},{24,32},{28,36},{32,40... | collective-permute-start | bytes 1769480 | tf_op jit(solution)/shard_map/ppermute | solution.py:10
  387.5 19.6 %collective-permute-start.6 = (f32[2,1,192,384]{3,2,1,0:T(8,128)S(1)}, f32[2,1,192,384]{3,2,1,0:T(8,128)S(1)}, u32[]{:S(2)}, u32[]{:S(2)}) collective-permute-start(f32[2,1,192,384]{3,2,1,0:T(8,128)S(1)} %pad_maximum_fusion.2), channel_id=1, source_target_pairs={{16,0},{20,4},{24,8},{28,12},{32,16},{36,20},{40,24},{44,28},{48,3... | collective-permute-start | bytes 1769480 | tf_op jit(solution)/shard_map/ppermute | solution.py:10
  388.8 31.1 %collective-permute-start.5 = (f32[2,1,192,384]{3,2,1,0:T(8,128)S(1)}, f32[2,1,192,384]{3,2,1,0:T(8,128)S(1)}, u32[]{:S(2)}, u32[]{:S(2)}) collective-permute-start(f32[2,1,192,384]{3,2,1,0:T(8,128)S(1)} %pad_maximum_fusion.2), channel_id=1, source_target_pairs={{0,16},{4,20},{8,24},{12,28},{16,32},{20,36},{24,40},{28,44},{32,4... | collective-permute-start | bytes 1769480 | tf_op jit(solution)/shard_map/ppermute | solution.py:10
  534.9 17.3 %collective-permute-start.8 = (f32[2,1,192,384]{3,2,1,0:T(8,128)S(1)}, f32[2,1,192,384]{3,2,1,0:T(8,128)S(1)}, u32[]{:S(2)}, u32[]{:S(2)}) collective-permute-start(f32[2,1,192,384]{3,2,1,0:T(8,128)S(1)} %pad_maximum_fusion.3), channel_id=1, source_target_pairs={{32,0},{36,4},{40,8},{44,12},{48,16},{52,20},{56,24},{60,28},{64,3... | collective-permute-start | bytes 1769480 | tf_op jit(solution)/shard_map/ppermute | solution.py:10
  536.2 17.2 %collective-permute-start.7 = (f32[2,1,192,384]{3,2,1,0:T(8,128)S(1)}, f32[2,1,192,384]{3,2,1,0:T(8,128)S(1)}, u32[]{:S(2)}, u32[]{:S(2)}) collective-permute-start(f32[2,1,192,384]{3,2,1,0:T(8,128)S(1)} %pad_maximum_fusion.3), channel_id=1, source_target_pairs={{0,32},{4,36},{8,40},{12,44},{16,48},{20,52},{24,56},{28,60},{32,6... | collective-permute-start | bytes 1769480 | tf_op jit(solution)/shard_map/ppermute | solution.py:10
  668.4 34.6 %collective-permute-start.10 = (f32[2,1,192,384]{3,2,1,0:T(8,128)S(1)}, f32[2,1,192,384]{3,2,1,0:T(8,128)S(1)}, u32[]{:S(2)}, u32[]{:S(2)}) collective-permute-start(f32[2,1,192,384]{3,2,1,0:T(8,128)S(1)} %pad_maximum_fusion.4), channel_id=1, source_target_pairs={{64,0},{68,4},{72,8},{76,12},{80,16},{84,20},{88,24},{92,28},{96,3... | collective-permute-start | bytes 1769480 | tf_op jit(solution)/shard_map/ppermute | solution.py:10
  669.7 33.5 %collective-permute-start.9 = (f32[2,1,192,384]{3,2,1,0:T(8,128)S(1)}, f32[2,1,192,384]{3,2,1,0:T(8,128)S(1)}, u32[]{:S(2)}, u32[]{:S(2)}) collective-permute-start(f32[2,1,192,384]{3,2,1,0:T(8,128)S(1)} %pad_maximum_fusion.4), channel_id=1, source_target_pairs={{0,64},{4,68},{8,72},{12,76},{16,80},{20,84},{24,88},{28,92},{32,9... | collective-permute-start | bytes 1769480 | tf_op jit(solution)/shard_map/ppermute | solution.py:10
  818.2 23.4 %collective-permute-start.12 = (f32[2,1,192,384]{3,2,1,0:T(8,128)S(1)}, f32[2,1,192,384]{3,2,1,0:T(8,128)S(1)}, u32[]{:S(2)}, u32[]{:S(2)}) collective-permute-start(f32[2,1,192,384]{3,2,1,0:T(8,128)S(1)} %pad_maximum_fusion.5), channel_id=1, source_target_pairs={{128,0},{132,4},{136,8},{140,12},{144,16},{148,20},{152,24},{156,2... | collective-permute-start | bytes 1769480 | tf_op jit(solution)/shard_map/ppermute | solution.py:10
  819.5 35.7 %collective-permute-start.11 = (f32[2,1,192,384]{3,2,1,0:T(8,128)S(1)}, f32[2,1,192,384]{3,2,1,0:T(8,128)S(1)}, u32[]{:S(2)}, u32[]{:S(2)}) collective-permute-start(f32[2,1,192,384]{3,2,1,0:T(8,128)S(1)} %pad_maximum_fusion.5), channel_id=1, source_target_pairs={{0,128},{4,132},{8,136},{12,140},{16,144},{20,148},{24,152},{28,15... | collective-permute-start | bytes 1769480 | tf_op jit(solution)/shard_map/ppermute | solution.py:10
  964.2 2.5 copy-start.2
  997.7 3.5 copy-start
  1004.0 0.9 copy-start.1
Sparse Core Ops, SparseCore 0:
  966.8 30.8 all-gather.2
where the time goes:
time: 1020 us; the launch traced here: 1010 us
  other arithmetic  695 us (68%)
  waiting for transfers between devices  133 us (13%)
  matrix products  80.4 us (8%)
  starting transfers between devices  55.3 us (5%)
  between operations  37.5 us (4%)
  local copies, waits for them, and re-layouts  12.5 us (1%)
    another operation x49, other arithmetic, invert(): imag_factor = jnp.linalg.cholesky(imag_part)  201 us
    another operation x49, other arithmetic, invert(): square_factor = jnp.linalg.cholesky(squared)  201 us
    another operation x28, other arithmetic, invert(): jax.scipy.linalg.cho_solve((square_factor, True), factor_inverse)  141 us
    another operation x30, other arithmetic, invert(): jax.scipy.linalg.solve_triangular(imag_factor, identity, lower=True)  140 us
    ppermute x13, waiting for transfers between devices, shifted(): lax.ppermute(value, axis, [(source, source + steps) for source in range(f...  102 us
    ppermute x13, starting transfers between devices, shifted(): lax.ppermute(value, axis, [(source, source + steps) for source in range(f...  55.2 us
    dot_general x48, matrix products, complex_product(): return jnp.einsum('...ij,...jk->...ik', left, stacked, precision=high)  39.3 us
    all_gather x1, waiting for transfers between devices, shards(): lax.all_gather(green_local[:, None], 'energy', axis=0, tiled=True)[:, 0]  30.9 us
  transfers between devices with their start and end apart: 14, of which 12 were waited for; matrix products, arithmetic and copies ran while one was open for 11% of the time, Pallas kernels for 0%

commit v1 on v0

--- a/solution.py
+++ b/solution.py
@@ -2,6 +2,27 @@
 import jax.numpy as jnp
 from jax import lax
 from jax.sharding import PartitionSpec as P
+
+
+def ring_gather(array, axis, dim):
+    length, here, span = (lax.axis_size(axis), lax.axis_index(axis), array.shape[dim])
+    right = [(i, (i + 1) % length) for i in range(length)]
+    left = [(i, (i - 1) % length) for i in range(length)]
+    whole = jnp.zeros((*array.shape[:dim], length * span, *array.shape[dim + 1 :]), array.dtype)
+    whole = lax.dynamic_update_slice_in_dim(whole, array, here * span, axis=dim)
+    from_left = from_right = array
+    halfway = length // 2
+    for step in range(1, halfway + 1):
+        from_left = lax.ppermute(from_left, axis, right)
+        whole = lax.dynamic_update_slice_in_dim(
+            whole, from_left, (here - step) % length * span, axis=dim
+        )
+        if step < length - halfway:
+            from_right = lax.ppermute(from_right, axis, left)
+            whole = lax.dynamic_update_slice_in_dim(
+                whole, from_right, (here + step) % length * span, axis=dim
+            )
+    return whole
 
 
 def shifted(value, axis, steps):
@@ -105,7 +126,7 @@
     upper_all = jnp.broadcast_to(upper_one, (energy_count, block_width, 2 * block_width))
     lower_all = jnp.broadcast_to(lower_one, (energy_count, block_width, 2 * block_width))
     green_local = reduce_levels(matrix, lower_all, upper_all)
-    everyone = lax.all_gather(green_local[:, None], "energy", axis=0, tiled=True)[:, 0]
+    everyone = ring_gather(green_local[:, None], "energy", 0)[:, 0]
     pair_count = energy_pairs.shape[1]
     first = jnp.take(everyone, energy_pairs[:, :, 0], axis=0)
     second = jnp.take(everyone, energy_pairs[:, :, 1], axis=0)

time: 1020 us -> 993 us (0.974)
  waiting for transfers between devices: 133 us -> 114 us
  between operations: 37.5 us -> 24.2 us
    all_gather x1 -> x0, waiting for transfers between devices: 30.9 us -> none  [shards(): lax.all_gather(green_local[:, None], 'energy', axis=0, tiled=True)[:, 0]]
    ppermute x0 -> x3, waiting for transfers between devices: none -> 12.2 us  [the longest x2 12.2 us: ring_gather(): from_left = lax.ppermute(from_left, axis, right)]
  transfers between devices with their start and end apart: 14 -> 16, of which waited for: 12 -> 13; matrix products, arithmetic and copies ran while one was open for 11% -> 11% of each run, Pallas kernels for 0% -> 0%
where the time goes in v1:
time: 993 us; the launch traced here: 983 us
  other arithmetic  695 us (70%)
  waiting for transfers between devices  114 us (11%)
  matrix products  79.7 us (8%)
  starting transfers between devices  58.9 us (6%)
  between operations  24.2 us (2%)
  local copies, waits for them, and re-layouts  11.3 us (1%)
    another operation x49, other arithmetic, invert(): imag_factor = jnp.linalg.cholesky(imag_part)  201 us
    another operation x49, other arithmetic, invert(): square_factor = jnp.linalg.cholesky(squared)  201 us
    another operation x28, other arithmetic, invert(): jax.scipy.linalg.cho_solve((square_factor, True), factor_inverse)  141 us
    another operation x30, other arithmetic, invert(): jax.scipy.linalg.solve_triangular(imag_factor, identity, lower=True)  140 us
    ppermute x13, waiting for transfers between devices, shifted(): lax.ppermute(value, axis, [(source, source + steps) for source in range(f...  102 us
    ppermute x13, starting transfers between devices, shifted(): lax.ppermute(value, axis, [(source, source + steps) for source in range(f...  55.3 us
    dot_general x48, matrix products, complex_product(): return jnp.einsum('...ij,...jk->...ik', left, stacked, precision=high)  38.6 us
  transfers between devices with their start and end apart: 16, of which 13 were waited for; matrix products, arithmetic and copies ran while one was open for 11% of the time, Pallas kernels for 0%

profile of v1, /device:TPU:2, one launch (start us, length us, event | category | flops | bytes accessed | tf_op | source)
XLA Modules:
  0.0 982.7 jit_solution(16893173767106023227)
XLA Ops:
  6.8 11.7 %custom-call.81 = f32[1,128,128]{2,1,0:T(8,128)S(1)} custom-call(f32[1,128,128]{2,1,0:T(8,128)S(1)} %copy.15), custom_call_target="Cholesky" | custom-call | tf_op jit(solution)/shard_map/jit(cholesky)/cholesky | solution.py:57
  37.5 19.9 %custom-call.84 = f32[2,128,128]{1,2,0:T(8,128)S(1)} custom-call(f32[2,128,128]{2,1,0:T(8,128)S(1)} %pad_maximum_fusion.34), custom_call_target="InvertDiagBlocksLowerTriangular" | custom-call | tf_op jit(solution)/shard_map/jit(_solve_triangular)/triangular_solve/custom-call.1 | solution.py:58
  60.3 11.7 %custom-call.85 = f32[1,128,128]{2,1,0:T(8,128)S(1)} custom-call(f32[1,128,128]{2,1,0:T(8,128)S(1)} %cholesky.1192), custom_call_target="Cholesky" | custom-call | tf_op jit(solution)/shard_map/jit(cholesky)/cholesky | solution.py:65
  90.9 20.1 %custom-call.88 = f32[2,128,128]{1,2,0:T(8,128)S(1)} custom-call(f32[2,128,128]{2,1,0:T(8,128)S(1)} %pad_maximum_fusion.35), custom_call_target="InvertDiagBlocksLowerTriangular" | custom-call | tf_op jit(solution)/shard_map/jit(_cho_solve)/triangular_solve | solution.py:66
  134.8 11.7 %custom-call.90 = f32[1,128,128]{2,1,0:T(8,128)S(1)} custom-call(f32[1,128,128]{2,1,0:T(8,128)S(1)} %copy.29), custom_call_target="Cholesky" | custom-call | tf_op jit(solution)/shard_map/jit(cholesky)/cholesky | solution.py:57
  165.7 19.9 %custom-call.93 = f32[2,128,128]{1,2,0:T(8,128)S(1)} custom-call(f32[2,128,128]{2,1,0:T(8,128)S(1)} %pad_maximum_fusion.36), custom_call_target="InvertDiagBlocksLowerTriangular" | custom-call | tf_op jit(solution)/shard_map/jit(_solve_triangular)/triangular_solve/custom-call.1 | solution.py:58
  188.5 11.7 %custom-call.94 = f32[1,128,128]{2,1,0:T(8,128)S(1)} custom-call(f32[1,128,128]{2,1,0:T(8,128)S(1)} %cholesky.1198), custom_call_target="Cholesky" | custom-call | tf_op jit(solution)/shard_map/jit(cholesky)/cholesky | solution.py:65
  219.1 20.1 %custom-call.97 = f32[2,128,128]{1,2,0:T(8,128)S(1)} custom-call(f32[2,128,128]{2,1,0:T(8,128)S(1)} %pad_maximum_fusion.37), custom_call_target="InvertDiagBlocksLowerTriangular" | custom-call | tf_op jit(solution)/shard_map/jit(_cho_solve)/triangular_solve | solution.py:66
  268.3 11.7 %custom-call.99 = f32[1,128,128]{2,1,0:T(8,128)S(1)} custom-call(f32[1,128,128]{2,1,0:T(8,128)S(1)} %copy.43), custom_call_target="Cholesky" | custom-call | tf_op jit(solution)/shard_map/jit(cholesky)/cholesky | solution.py:57
  299.2 19.9 %custom-call.102 = f32[2,128,128]{1,2,0:T(8,128)S(1)} custom-call(f32[2,128,128]{2,1,0:T(8,128)S(1)} %pad_maximum_fusion.38), custom_call_target="InvertDiagBlocksLowerTriangular" | custom-call | tf_op jit(solution)/shard_map/jit(_solve_triangular)/triangular_solve/custom-call.1 | solution.py:58
  322.0 11.7 %custom-call.103 = f32[1,128,128]{2,1,0:T(8,128)S(1)} custom-call(f32[1,128,128]{2,1,0:T(8,128)S(1)} %cholesky.1204), custom_call_target="Cholesky" | custom-call | tf_op jit(solution)/shard_map/jit(cholesky)/cholesky | solution.py:65
  352.6 20.1 %custom-call.106 = f32[2,128,128]{1,2,0:T(8,128)S(1)} custom-call(f32[2,128,128]{2,1,0:T(8,128)S(1)} %pad_maximum_fusion.39), custom_call_target="InvertDiagBlocksLowerTriangular" | custom-call | tf_op jit(solution)/shard_map/jit(_cho_solve)/triangular_solve | solution.py:66
  400.7 12.6 %collective-permute-done.5 = f32[2,1,192,384]{3,2,1,0:T(8,128)S(1)} collective-permute-done((f32[2,1,192,384]{3,2,1,0:T(8,128)S(1)}, f32[2,1,192,384]{3,2,1,0:T(8,128)S(1)}, u32[]{:S(2)}, u32[]{:S(2)}) %collective-permute-start.5) | collective-permute-done | bytes 589856 | tf_op jit(solution)/shard_map/ppermute | solution.py:31
  415.8 11.7 %custom-call.108 = f32[1,128,128]{2,1,0:T(8,128)S(1)} custom-call(f32[1,128,128]{2,1,0:T(8,128)S(1)} %copy.57), custom_call_target="Cholesky" | custom-call | tf_op jit(solution)/shard_map/jit(cholesky)/cholesky | solution.py:57
  446.6 19.9 %custom-call.111 = f32[2,128,128]{1,2,0:T(8,128)S(1)} custom-call(f32[2,128,128]{2,1,0:T(8,128)S(1)} %pad_maximum_fusion.40), custom_call_target="InvertDiagBlocksLowerTriangular" | custom-call | tf_op jit(solution)/shard_map/jit(_solve_triangular)/triangular_solve/custom-call.1 | solution.py:58
  469.4 11.7 %custom-call.112 = f32[1,128,128]{2,1,0:T(8,128)S(1)} custom-call(f32[1,128,128]{2,1,0:T(8,128)S(1)} %cholesky.1210), custom_call_target="Cholesky" | custom-call | tf_op jit(solution)/shard_map/jit(cholesky)/cholesky | solution.py:65
  500.0 20.1 %custom-call.115 = f32[2,128,128]{1,2,0:T(8,128)S(1)} custom-call(f32[2,128,128]{2,1,0:T(8,128)S(1)} %pad_maximum_fusion.41), custom_call_target="InvertDiagBlocksLowerTriangular" | custom-call | tf_op jit(solution)/shard_map/jit(_cho_solve)/triangular_solve | solution.py:66
  549.3 11.7 %custom-call.117 = f32[1,128,128]{2,1,0:T(8,128)S(1)} custom-call(f32[1,128,128]{2,1,0:T(8,128)S(1)} %copy.71), custom_call_target="Cholesky" | custom-call | tf_op jit(solution)/shard_map/jit(cholesky)/cholesky | solution.py:57
  580.1 19.9 %custom-call.120 = f32[2,128,128]{1,2,0:T(8,128)S(1)} custom-call(f32[2,128,128]{2,1,0:T(8,128)S(1)} %pad_maximum_fusion.42), custom_call_target="InvertDiagBlocksLowerTriangular" | custom-call | tf_op jit(solution)/shard_map/jit(_solve_triangular)/triangular_solve/custom-call.1 | solution.py:58
  602.9 11.7 %custom-call.121 = f32[1,128,128]{2,1,0:T(8,128)S(1)} custom-call(f32[1,128,128]{2,1,0:T(8,128)S(1)} %cholesky.1216), custom_call_target="Cholesky" | custom-call | tf_op jit(solution)/shard_map/jit(cholesky)/cholesky | solution.py:65
  633.5 20.1 %custom-call.124 = f32[2,128,128]{1,2,0:T(8,128)S(1)} custom-call(f32[2,128,128]{2,1,0:T(8,128)S(1)} %pad_maximum_fusion.43), custom_call_target="InvertDiagBlocksLowerTriangular" | custom-call | tf_op jit(solution)/shard_map/jit(_cho_solve)/triangular_solve | solution.py:66
  673.5 23.0 %collective-permute-done.10 = f32[2,1,192,384]{3,2,1,0:T(8,128)S(1)} collective-permute-done((f32[2,1,192,384]{3,2,1,0:T(8,128)S(1)}, f32[2,1,192,384]{3,2,1,0:T(8,128)S(1)}, u32[]{:S(2)}, u32[]{:S(2)}) %collective-permute-start.10) | collective-permute-done | bytes 589856 | tf_op jit(solution)/shard_map/ppermute | solution.py:31
  699.1 11.7 %custom-call.126 = f32[1,128,128]{2,1,0:T(8,128)S(1)} custom-call(f32[1,128,128]{2,1,0:T(8,128)S(1)} %copy.85), custom_call_target="Cholesky" | custom-call | tf_op jit(solution)/shard_map/jit(cholesky)/cholesky | solution.py:57
  729.9 19.9 %custom-call.129 = f32[2,128,128]{1,2,0:T(8,128)S(1)} custom-call(f32[2,128,128]{2,1,0:T(8,128)S(1)} %pad_maximum_fusion.44), custom_call_target="InvertDiagBlocksLowerTriangular" | custom-call | tf_op jit(solution)/shard_map/jit(_solve_triangular)/triangular_solve/custom-call.1 | solution.py:58
  752.7 11.7 %custom-call.130 = f32[1,128,128]{2,1,0:T(8,128)S(1)} custom-call(f32[1,128,128]{2,1,0:T(8,128)S(1)} %cholesky.1222), custom_call_target="Cholesky" | custom-call | tf_op jit(solution)/shard_map/jit(cholesky)/cholesky | solution.py:65
  783.3 20.1 %custom-call.133 = f32[2,128,128]{1,2,0:T(8,128)S(1)} custom-call(f32[2,128,128]{2,1,0:T(8,128)S(1)} %pad_maximum_fusion.45), custom_call_target="InvertDiagBlocksLowerTriangular" | custom-call | tf_op jit(solution)/shard_map/jit(_cho_solve)/triangular_solve | solution.py:66
  813.0 12.9 %collective-permute-start.11 = (f32[2,1,192,384]{3,2,1,0:T(8,128)S(1)}, f32[2,1,192,384]{3,2,1,0:T(8,128)S(1)}, u32[]{:S(2)}, u32[]{:S(2)}) collective-permute-start(f32[2,1,192,384]{3,2,1,0:T(8,128)S(1)} %pad_maximum_fusion.5), channel_id=1, source_target_pairs={{0,128},{4,132},{8,136},{12,140},{16,144},{20,148},{24,152},{28,15... | collective-permute-start | bytes 1769480 | tf_op jit(solution)/shard_map/ppermute | solution.py:31
  835.3 13.5 %collective-permute-done.11 = f32[2,1,192,384]{3,2,1,0:T(8,128)S(1)} collective-permute-done((f32[2,1,192,384]{3,2,1,0:T(8,128)S(1)}, f32[2,1,192,384]{3,2,1,0:T(8,128)S(1)}, u32[]{:S(2)}, u32[]{:S(2)}) %collective-permute-start.11) | collective-permute-done | bytes 589856 | tf_op jit(solution)/shard_map/ppermute | solution.py:31
  851.1 11.7 %custom-call.135 = f32[1,128,128]{2,1,0:T(8,128)S(1)} custom-call(f32[1,128,128]{2,1,0:T(8,128)S(1)} %cholesky.1225), custom_call_target="Cholesky" | custom-call | tf_op jit(solution)/shard_map/jit(cholesky)/cholesky | solution.py:57
  881.9 19.9 %custom-call.138 = f32[2,128,128]{1,2,0:T(8,128)S(1)} custom-call(f32[2,128,128]{2,1,0:T(8,128)S(1)} %pad_maximum_fusion.46), custom_call_target="InvertDiagBlocksLowerTriangular" | custom-call | tf_op jit(solution)/shard_map/jit(_solve_triangular)/triangular_solve/custom-call.1 | solution.py:58
  904.4 11.7 %custom-call.139 = f32[1,128,128]{2,1,0:T(8,128)S(1)} custom-call(f32[1,128,128]{2,1,0:T(8,128)S(1)} %cholesky.1228), custom_call_target="Cholesky" | custom-call | tf_op jit(solution)/shard_map/jit(cholesky)/cholesky | solution.py:65
  935.0 19.9 %custom-call.142 = f32[2,128,128]{1,2,0:T(8,128)S(1)} custom-call(f32[2,128,128]{2,1,0:T(8,128)S(1)} %pad_maximum_fusion.47), custom_call_target="InvertDiagBlocksLowerTriangular" | custom-call | tf_op jit(solution)/shard_map/jit(_cho_solve)/triangular_solve | solution.py:66
  (568 shorter events, 453.0 us)
Async XLA Ops:
  1.7 114.7 %collective-permute-start = (f32[192,192]{0,1:T(8,128)S(1)}, f32[192,192]{0,1:T(8,128)S(1)}, u32[]{:S(2)}, u32[]{:S(2)}) collective-permute-start(f32[192,192]{0,1:T(8,128)S(1)} %get-tuple-element.293), channel_id=1, source_target_pairs={{0,4},{4,8},{8,12},{12,16},{16,20},{20,24},{24,28},{28,32},{32,36}... | collective-permute-start | bytes 442376 | tf_op jit(solution)/shard_map/ppermute | solution.py:31
  117.5 11.0 %collective-permute-start.2 = (f32[2,1,192,384]{3,2,1,0:T(8,128)S(1)}, f32[2,1,192,384]{3,2,1,0:T(8,128)S(1)}, u32[]{:S(2)}, u32[]{:S(2)}) collective-permute-start(f32[2,1,192,384]{3,2,1,0:T(8,128)S(1)} %pad_maximum_fusion), channel_id=1, source_target_pairs={{4,0},{8,4},{12,8},{16,12},{20,16},{24,20},{28,24},{32,28},{36,32}... | collective-permute-start | bytes 1769480 | tf_op jit(solution)/shard_map/ppermute | solution.py:31
  121.1 11.2 %collective-permute-start.1 = (f32[2,1,192,384]{3,2,1,0:T(8,128)S(1)}, f32[2,1,192,384]{3,2,1,0:T(8,128)S(1)}, u32[]{:S(2)}, u32[]{:S(2)}) collective-permute-start(f32[2,1,192,384]{3,2,1,0:T(8,128)S(1)} %pad_maximum_fusion), channel_id=1, source_target_pairs={{0,4},{4,8},{8,12},{12,16},{16,20},{20,24},{24,28},{28,32},{32,36}... | collective-permute-start | bytes 1769480 | tf_op jit(solution)/shard_map/ppermute | solution.py:31
  247.5 16.3 %collective-permute-start.4 = (f32[2,1,192,384]{3,2,1,0:T(8,128)S(1)}, f32[2,1,192,384]{3,2,1,0:T(8,128)S(1)}, u32[]{:S(2)}, u32[]{:S(2)}) collective-permute-start(f32[2,1,192,384]{3,2,1,0:T(8,128)S(1)} %pad_maximum_fusion.1), channel_id=1, source_target_pairs={{8,0},{12,4},{16,8},{20,12},{24,16},{28,20},{32,24},{36,28},{40,32... | collective-permute-start | bytes 1769480 | tf_op jit(solution)/shard_map/ppermute | solution.py:31
  249.4 16.5 %collective-permute-start.3 = (f32[2,1,192,384]{3,2,1,0:T(8,128)S(1)}, f32[2,1,192,384]{3,2,1,0:T(8,128)S(1)}, u32[]{:S(2)}, u32[]{:S(2)}) collective-permute-start(f32[2,1,192,384]{3,2,1,0:T(8,128)S(1)} %pad_maximum_fusion.1), channel_id=1, source_target_pairs={{0,8},{4,12},{8,16},{12,20},{16,24},{20,28},{24,32},{28,36},{32,40... | collective-permute-start | bytes 1769480 | tf_op jit(solution)/shard_map/ppermute | solution.py:31
  380.9 19.6 %collective-permute-start.6 = (f32[2,1,192,384]{3,2,1,0:T(8,128)S(1)}, f32[2,1,192,384]{3,2,1,0:T(8,128)S(1)}, u32[]{:S(2)}, u32[]{:S(2)}) collective-permute-start(f32[2,1,192,384]{3,2,1,0:T(8,128)S(1)} %pad_maximum_fusion.2), channel_id=1, source_target_pairs={{16,0},{20,4},{24,8},{28,12},{32,16},{36,20},{40,24},{44,28},{48,3... | collective-permute-start | bytes 1769480 | tf_op jit(solution)/shard_map/ppermute | solution.py:31
  382.2 31.1 %collective-permute-start.5 = (f32[2,1,192,384]{3,2,1,0:T(8,128)S(1)}, f32[2,1,192,384]{3,2,1,0:T(8,128)S(1)}, u32[]{:S(2)}, u32[]{:S(2)}) collective-permute-start(f32[2,1,192,384]{3,2,1,0:T(8,128)S(1)} %pad_maximum_fusion.2), channel_id=1, source_target_pairs={{0,16},{4,20},{8,24},{12,28},{16,32},{20,36},{24,40},{28,44},{32,4... | collective-permute-start | bytes 1769480 | tf_op jit(solution)/shard_map/ppermute | solution.py:31
  528.4 17.3 %collective-permute-start.8 = (f32[2,1,192,384]{3,2,1,0:T(8,128)S(1)}, f32[2,1,192,384]{3,2,1,0:T(8,128)S(1)}, u32[]{:S(2)}, u32[]{:S(2)}) collective-permute-start(f32[2,1,192,384]{3,2,1,0:T(8,128)S(1)} %pad_maximum_fusion.3), channel_id=1, source_target_pairs={{32,0},{36,4},{40,8},{44,12},{48,16},{52,20},{56,24},{60,28},{64,3... | collective-permute-start | bytes 1769480 | tf_op jit(solution)/shard_map/ppermute | solution.py:31
  529.7 17.2 %collective-permute-start.7 = (f32[2,1,192,384]{3,2,1,0:T(8,128)S(1)}, f32[2,1,192,384]{3,2,1,0:T(8,128)S(1)}, u32[]{:S(2)}, u32[]{:S(2)}) collective-permute-start(f32[2,1,192,384]{3,2,1,0:T(8,128)S(1)} %pad_maximum_fusion.3), channel_id=1, source_target_pairs={{0,32},{4,36},{8,40},{12,44},{16,48},{20,52},{24,56},{28,60},{32,6... | collective-permute-start | bytes 1769480 | tf_op jit(solution)/shard_map/ppermute | solution.py:31
  661.8 34.6 %collective-permute-start.10 = (f32[2,1,192,384]{3,2,1,0:T(8,128)S(1)}, f32[2,1,192,384]{3,2,1,0:T(8,128)S(1)}, u32[]{:S(2)}, u32[]{:S(2)}) collective-permute-start(f32[2,1,192,384]{3,2,1,0:T(8,128)S(1)} %pad_maximum_fusion.4), channel_id=1, source_target_pairs={{64,0},{68,4},{72,8},{76,12},{80,16},{84,20},{88,24},{92,28},{96,3... | collective-permute-start | bytes 1769480 | tf_op jit(solution)/shard_map/ppermute | solution.py:31
  663.1 33.5 %collective-permute-start.9 = (f32[2,1,192,384]{3,2,1,0:T(8,128)S(1)}, f32[2,1,192,384]{3,2,1,0:T(8,128)S(1)}, u32[]{:S(2)}, u32[]{:S(2)}) collective-permute-start(f32[2,1,192,384]{3,2,1,0:T(8,128)S(1)} %pad_maximum_fusion.4), channel_id=1, source_target_pairs={{0,64},{4,68},{8,72},{12,76},{16,80},{20,84},{24,88},{28,92},{32,9... | collective-permute-start | bytes 1769480 | tf_op jit(solution)/shard_map/ppermute | solution.py:31
  810.0 15.9 %copy-start.2 = (s32[1,8,2]{1,2,0:T(2,128)S(1)}, s32[1,8,2]{1,2,0:T(2,128)}, u32[]{:S(2)}) copy-start(s32[1,8,2]{1,2,0:T(2,128)} %param.20) | copy-start | bytes 196
  811.7 23.4 %collective-permute-start.12 = (f32[2,1,192,384]{3,2,1,0:T(8,128)S(1)}, f32[2,1,192,384]{3,2,1,0:T(8,128)S(1)}, u32[]{:S(2)}, u32[]{:S(2)}) collective-permute-start(f32[2,1,192,384]{3,2,1,0:T(8,128)S(1)} %pad_maximum_fusion.5), channel_id=1, source_target_pairs={{128,0},{132,4},{136,8},{140,12},{144,16},{148,20},{152,24},{156,2... | collective-permute-start | bytes 1769480 | tf_op jit(solution)/shard_map/ppermute | solution.py:31
  813.0 35.7 %collective-permute-start.11 = (f32[2,1,192,384]{3,2,1,0:T(8,128)S(1)}, f32[2,1,192,384]{3,2,1,0:T(8,128)S(1)}, u32[]{:S(2)}, u32[]{:S(2)}) collective-permute-start(f32[2,1,192,384]{3,2,1,0:T(8,128)S(1)} %pad_maximum_fusion.5), channel_id=1, source_target_pairs={{0,128},{4,132},{8,136},{12,140},{16,144},{20,148},{24,152},{28,15... | collective-permute-start | bytes 1769480 | tf_op jit(solution)/shard_map/ppermute | solution.py:31
  959.5 18.1 %copy-start = (f32[192,384]{1,0:T(8,128)}, f32[192,384]{1,0:T(8,128)S(1)}, u32[]{:S(2)}) copy-start(f32[192,384]{1,0:T(8,128)S(1)} %get-tuple-element.385) | copy-start | bytes 884740
  959.5 8.0 collective-permute-start.13
  961.2 6.7 collective-permute-start.14
  967.5 7.9 collective-permute-start.15
  980.4 0.9 copy-start.1
